TPU v7x, 32 devices: a whole 2x2x4 slice. The times are simulated.
32 devices in a mesh: rep: 2 (over y), seq: 4 (over x, core), head: 4 (over z).
Axes of the slice: x: 2, y: 2, z: 4, core: 2. Of those that a mesh axis runs over, the one named last changes fastest.
Arguments:
- queries: bfloat16 [2048, 4096], P(('rep', 'seq', 'head')), parts along dimension 0, may hold values from -6 to 6
- key_rows: bfloat16 [2048, 4096], P(('rep', 'seq', 'head')), parts along dimension 0, may hold values from -6 to 6
- value_rows: bfloat16 [2048, 4096], P(('rep', 'seq', 'head')), parts along dimension 0, may hold values from -6 to 6
- out_grad: bfloat16 [2048, 4096], P(('rep', 'seq', 'head')), parts along dimension 0, may hold values from -6 to 6
Outputs:
- attended: bfloat16 [2048, 4096], P(('rep', 'seq', 'head')), parts along dimension 0
- query_grad: bfloat16 [2048, 4096], P(('rep', 'seq', 'head')), parts along dimension 0
- key_grad: bfloat16 [2048, 4096], P(('rep', 'seq', 'head')), parts along dimension 0
- value_grad: bfloat16 [2048, 4096], P(('rep', 'seq', 'head')), parts along dimension 0
There are 2 independent parts, one for each index of `rep`. A program takes and returns all parts, laid end to end along the dimension named above; each array names one. Nothing has to cross between parts.
All inputs are finite; a program needn't handle non-finite values.
Results may differ from a plain program's by a relative error of at most 0.0049.
Values may be sent and summed in bfloat16 or wider, within the bound.
A program may use at most 64 MiB of HBM per device.

v0:
```python
import jax
import jax.numpy as jnp
from jax import lax
from jax.sharding import PartitionSpec as P

DH = 128
BLK_MAX = 512


def shards(queries, key_rows, value_rows, out_grad):
    f32 = jnp.float32
    bf16 = jnp.bfloat16
    head_count = lax.axis_size("head")
    tok_count = queries.shape[0]
    local_heads = queries.shape[1] // (head_count * DH)
    seq_rows = tok_count * head_count
    block = min(BLK_MAX, seq_rows)
    block_count = seq_rows // block
    factor = float(DH * seq_rows * lax.axis_size("seq")) ** (-0.5)

    def to_heads(matrix):
        return matrix.reshape(tok_count, head_count, local_heads, DH)

    def per_head(parts):
        heads_here = parts[0].shape[2]
        query_blocks, key_blocks, value_blocks, grad_blocks = (
            item.reshape(block_count, block, heads_here, DH) for item in parts
        )
        kv_state = jnp.einsum(
            "bthd,bthe->bhde", key_blocks, value_blocks, preferred_element_type=f32
        )
        grad_state = jnp.einsum(
            "bthd,bthe->bhde", query_blocks, grad_blocks, preferred_element_type=f32
        )
        empty_state = jnp.zeros((1, heads_here, DH, DH), f32)
        local_prefix = jnp.concatenate([empty_state, jnp.cumsum(kv_state, 0)[:-1]], 0)
        tail_sums = jnp.cumsum(grad_state[::-1], 0)[::-1]
        local_suffix = jnp.concatenate([tail_sums[1:], empty_state], 0)
        kv_total = jnp.sum(kv_state, 0)
        grad_total = jnp.sum(grad_state, 0)
        my_index = lax.axis_index("seq")
        pieces = (
            lax.all_gather(kv_total[None], "seq", axis=0, tiled=True),
            lax.all_gather(grad_total[None], "seq", axis=0, tiled=True),
        )
        count = pieces[0].shape[0]
        index = jnp.arange(count, dtype=jnp.int32)
        below_me = (index < my_index).astype(f32)[:, None, None, None]
        above_me = (index > my_index).astype(f32)[:, None, None, None]
        span_prefix = jnp.sum(pieces[0] * below_me, 0)
        span_suffix = jnp.sum(pieces[1] * above_me, 0)
        prefix = (local_prefix + span_prefix[None]).astype(bf16)
        suffix = (local_suffix + span_suffix[None]).astype(bf16)
        causal = (jnp.arange(block)[:, None] >= jnp.arange(block)[None, :])[None, None]
        scores = jnp.einsum("bthd,bshd->bhts", query_blocks, key_blocks, preferred_element_type=f32)
        scores = jnp.where(causal, scores * factor, 0.0).astype(bf16)
        attended = jnp.einsum("bhts,bshd->bthd", scores, value_blocks, preferred_element_type=f32)
        attended = attended + factor * jnp.einsum(
            "bthd,bhde->bthe", query_blocks, prefix, preferred_element_type=f32
        )
        dscores = jnp.einsum(
            "bthe,bshe->bhts", grad_blocks, value_blocks, preferred_element_type=f32
        )
        dscores = jnp.where(causal, dscores * factor, 0.0).astype(bf16)
        query_grad = jnp.einsum("bhts,bshd->bthd", dscores, key_blocks, preferred_element_type=f32)
        query_grad = query_grad + factor * jnp.einsum(
            "bthe,bhde->bthd", grad_blocks, prefix, preferred_element_type=f32
        )
        key_grad = jnp.einsum("bhts,bthd->bshd", dscores, query_blocks, preferred_element_type=f32)
        key_grad = key_grad + factor * jnp.einsum(
            "bshe,bhde->bshd", value_blocks, suffix, preferred_element_type=f32
        )
        value_grad = jnp.einsum("bhts,bthe->bshe", scores, grad_blocks, preferred_element_type=f32)
        value_grad = value_grad + factor * jnp.einsum(
            "bshd,bhde->bshe", key_blocks, suffix, preferred_element_type=f32
        )
        results = tuple(
            (
                item.astype(bf16).reshape(seq_rows, 1, heads_here, DH)
                for item in (attended, query_grad, key_grad, value_grad)
            )
        )
        return (
            lax.all_to_all(results[0], "head", split_axis=0, concat_axis=1, tiled=True),
            lax.all_to_all(results[1], "head", split_axis=0, concat_axis=1, tiled=True),
            lax.all_to_all(results[2], "head", split_axis=0, concat_axis=1, tiled=True),
            lax.all_to_all(results[3], "head", split_axis=0, concat_axis=1, tiled=True),
        )

    outputs = per_head(
        (
            lax.all_to_all(to_heads(queries), "head", split_axis=1, concat_axis=0, tiled=True),
            lax.all_to_all(to_heads(key_rows), "head", split_axis=1, concat_axis=0, tiled=True),
            lax.all_to_all(to_heads(value_rows), "head", split_axis=1, concat_axis=0, tiled=True),
            lax.all_to_all(to_heads(out_grad), "head", split_axis=1, concat_axis=0, tiled=True),
        )
    )
    return tuple((item.reshape(tok_count, queries.shape[1]) for item in outputs))


def solution(mesh):
    placed = (
        P(("rep", "seq", "head"), None),
        P(("rep", "seq", "head"), None),
        P(("rep", "seq", "head"), None),
        P(("rep", "seq", "head"), None),
    )
    return jax.shard_map(
        shards,
        mesh=mesh,
        in_specs=placed,
        out_specs=(
            P(("rep", "seq", "head"), None),
            P(("rep", "seq", "head"), None),
            P(("rep", "seq", "head"), None),
            P(("rep", "seq", "head"), None),
        ),
        check_vma=False,
    )
```

profile of v0, /device:TPU:0, one launch (start us, length us, event | category | flops | bytes accessed | tf_op | source)
XLA Modules:
  0.0 174.0 jit_solution(1147366358603336593)
XLA Ops:
  7.2 0.0 copy-start.4
  7.2 1.2 copy.85
  8.4 1.0 copy.50
  9.4 6.3 %all-to-all-start.1 = ((bf16[64,4,8,128]{3,0,2,1:T(8,128)(2,1)}), bf16[64,4,8,128]{3,0,2,1:T(8,128)(2,1)S(1)}, u32[]{:S(2)}, u32[]{:S(2)}) async-start(bf16[64,4,8,128]{3,0,2,1:T(8,128)(2,1)} %copy.50), calls=%async_computation.1 | async-start | bytes 1048576 | tf_op jit(solution)/shard_map/all_to_all | solution.py:93
  15.7 0.0 copy-done.4
  15.7 0.1 copy.86
  15.8 1.0 copy.52
  16.8 13.4 %all-to-all-done.1 = bf16[64,4,8,128]{3,0,2,1:T(8,128)(2,1)S(1)} async-done(((bf16[64,4,8,128]{3,0,2,1:T(8,128)(2,1)}), bf16[64,4,8,128]{3,0,2,1:T(8,128)(2,1)S(1)}, u32[]{:S(2)}, u32[]{:S(2)}) %all-to-all-start.1) | async-done | bytes 524320 | tf_op jit(solution)/shard_map/all_to_all | solution.py:93
  30.2 3.5 %all-to-all-start.2 = ((bf16[64,4,8,128]{3,0,2,1:T(8,128)(2,1)}), bf16[64,4,8,128]{3,0,2,1:T(8,128)(2,1)S(1)}, u32[]{:S(2)}, u32[]{:S(2)}) async-start(bf16[64,4,8,128]{3,0,2,1:T(8,128)(2,1)} %copy.52), calls=%async_computation.2 | async-start | bytes 1048576 | tf_op jit(solution)/shard_map/all_to_all | solution.py:94
  33.7 0.0 all-gather.5.cloned.1.call-start
  33.7 0.0 copy-start.5
  33.8 13.9 %all-to-all-done.2 = bf16[64,4,8,128]{3,0,2,1:T(8,128)(2,1)S(1)} async-done(((bf16[64,4,8,128]{3,0,2,1:T(8,128)(2,1)}), bf16[64,4,8,128]{3,0,2,1:T(8,128)(2,1)S(1)}, u32[]{:S(2)}, u32[]{:S(2)}) %all-to-all-start.2) | async-done | bytes 524320 | tf_op jit(solution)/shard_map/all_to_all | solution.py:94
  47.7 1.1 fusion.16
  48.8 0.0 all-gather.5.cloned.1.call-update
  48.8 0.0 copy-done.5
  48.8 0.1 copy.84
  48.9 1.0 copy.48
  49.9 3.5 %all-to-all-start = ((bf16[64,4,8,128]{3,0,2,1:T(8,128)(2,1)}), bf16[64,4,8,128]{3,0,2,1:T(8,128)(2,1)S(1)}, u32[]{:S(2)}, u32[]{:S(2)}) async-start(bf16[64,4,8,128]{3,0,2,1:T(8,128)(2,1)} %copy.48), calls=%async_computation | async-start | bytes 1048576 | tf_op jit(solution)/shard_map/all_to_all | solution.py:92
  53.4 0.0 copy-done.6
  53.4 0.1 copy.87
  53.5 1.0 copy.59
  54.5 12.8 %all-to-all-done = bf16[64,4,8,128]{3,0,2,1:T(8,128)(2,1)S(1)} async-done(((bf16[64,4,8,128]{3,0,2,1:T(8,128)(2,1)}), bf16[64,4,8,128]{3,0,2,1:T(8,128)(2,1)S(1)}, u32[]{:S(2)}, u32[]{:S(2)}) %all-to-all-start) | async-done | bytes 524320 | tf_op jit(solution)/shard_map/all_to_all | solution.py:92
  67.4 3.5 %all-to-all-start.4 = ((bf16[64,4,8,128]{3,0,2,1:T(8,128)(2,1)}), bf16[64,4,8,128]{3,0,2,1:T(8,128)(2,1)S(1)}, u32[]{:S(2)}, u32[]{:S(2)}) async-start(bf16[64,4,8,128]{3,0,2,1:T(8,128)(2,1)} %copy.59), calls=%async_computation.4 | async-start | bytes 1048576 | tf_op jit(solution)/shard_map/all_to_all | solution.py:95
  70.8 0.0 all-gather.7.cloned.1.call-start
  70.9 13.9 %all-to-all-done.4 = bf16[64,4,8,128]{3,0,2,1:T(8,128)(2,1)S(1)} async-done(((bf16[64,4,8,128]{3,0,2,1:T(8,128)(2,1)}), bf16[64,4,8,128]{3,0,2,1:T(8,128)(2,1)S(1)}, u32[]{:S(2)}, u32[]{:S(2)}) %all-to-all-start.4) | async-done | bytes 524320 | tf_op jit(solution)/shard_map/all_to_all | solution.py:95
  84.8 1.1 fusion.17
  86.0 0.0 all-gather.7.cloned.1.call-update
  86.1 0.4 select_convert_fusion.1
  86.5 1.4 convolution_bitcast_fusion.3
  87.9 1.9 %multiply_reduce_fusion.1 = bf16[8,128,128]{2,1,0:T(8,128)(2,1)S(1)} fusion(f32[4,8,128,128]{3,2,1,0:T(8,128)} %bitcast.130, f32[4]{0:T(128)S(1)} %compare_convert_fusion.1), kind=kLoop, calls=%fused_computation.2 | loop fusion | flops 917504 | bytes 2359312 | tf_op jit(solution)/shard_map/reduce_sum | solution.py:50
  89.9 0.0 copy-done.1
  89.9 0.3 fusion.9
  90.2 1.1 copy.57
  91.3 4.1 %all-to-all-start.3 = ((bf16[256,1,8,128]{3,2,1,0:T(8,128)(2,1)}), bf16[256,1,8,128]{3,2,1,0:T(8,128)(2,1)}, u32[]{:S(2)}, u32[]{:S(2)}) async-start(bf16[256,1,8,128]{3,2,1,0:T(8,128)(2,1)} %copy.57), calls=%async_computation.3 | async-start | bytes 1048576 | tf_op jit(solution)/shard_map/all_to_all | solution.py:84
  95.5 1.5 convolution_bitcast_fusion
  96.9 10.9 %all-gather.7.cloned.1.call-done = f32[32,128,128]{2,1,0:T(8,128)} async-done(((f32[8,128,128]{2,1,0:T(8,128)}), f32[32,128,128]{2,1,0:T(8,128)}) %all-gather.7.cloned.1.call-update) | async-done | bytes 2097168 | tf_op jit(solution)/shard_map/all_gather | solution.py:44
  107.9 1.9 %multiply_reduce_fusion = bf16[8,128,128]{2,1,0:T(8,128)(2,1)S(1)} fusion(f32[4,8,128,128]{3,2,1,0:T(8,128)} %bitcast.131, f32[4]{0:T(128)S(1)} %compare_convert_fusion), kind=kLoop, calls=%fused_computation | loop fusion | flops 917504 | bytes 2359312 | tf_op jit(solution)/shard_map/reduce_sum | solution.py:51
  109.7 0.0 copy-start.2
  109.7 0.3 fusion.8
  110.0 0.4 copy-done.2
  110.4 1.1 copy.72
  111.6 0.0 all-to-all-done.3
  111.6 4.6 %all-to-all-start.7 = ((bf16[256,1,8,128]{3,2,1,0:T(8,128)(2,1)}), bf16[256,1,8,128]{3,2,1,0:T(8,128)(2,1)}, u32[]{:S(2)}, u32[]{:S(2)}) async-start(bf16[256,1,8,128]{3,2,1,0:T(8,128)(2,1)} %copy.72), calls=%async_computation.7 | async-start | bytes 1048576 | tf_op jit(solution)/shard_map/all_to_all | solution.py:87
  116.2 0.4 select_convert_fusion
  116.6 0.5 convolution_bitcast_fusion.1
  117.1 0.0 copy-done.3
  117.1 0.3 fusion.10
  117.4 1.1 copy.67
  118.6 12.6 %all-to-all-done.7 = bf16[256,1,8,128]{3,2,1,0:T(8,128)(2,1)} async-done(((bf16[256,1,8,128]{3,2,1,0:T(8,128)(2,1)}), bf16[256,1,8,128]{3,2,1,0:T(8,128)(2,1)}, u32[]{:S(2)}, u32[]{:S(2)}) %all-to-all-start.7) | async-done | bytes 524320 | tf_op jit(solution)/shard_map/all_to_all | solution.py:87
  131.2 3.5 %all-to-all-start.6 = ((bf16[256,1,8,128]{3,2,1,0:T(8,128)(2,1)}), bf16[256,1,8,128]{3,2,1,0:T(8,128)(2,1)S(1)}, u32[]{:S(2)}, u32[]{:S(2)}) async-start(bf16[256,1,8,128]{3,2,1,0:T(8,128)(2,1)} %copy.67), calls=%async_computation.6 | async-start | bytes 1048576 | tf_op jit(solution)/shard_map/all_to_all | solution.py:86
  134.6 0.4 convolution_bitcast_fusion.2
  135.1 0.3 fusion.11
  135.4 1.1 copy.62
  136.5 12.1 %all-to-all-done.6 = bf16[256,1,8,128]{3,2,1,0:T(8,128)(2,1)S(1)} async-done(((bf16[256,1,8,128]{3,2,1,0:T(8,128)(2,1)}), bf16[256,1,8,128]{3,2,1,0:T(8,128)(2,1)S(1)}, u32[]{:S(2)}, u32[]{:S(2)}) %all-to-all-start.6) | async-done | bytes 524320 | tf_op jit(solution)/shard_map/all_to_all | solution.py:86
  148.7 3.5 %all-to-all-start.5 = ((bf16[256,1,8,128]{3,2,1,0:T(8,128)(2,1)}), bf16[256,1,8,128]{3,2,1,0:T(8,128)(2,1)S(1)}, u32[]{:S(2)}, u32[]{:S(2)}) async-start(bf16[256,1,8,128]{3,2,1,0:T(8,128)(2,1)} %copy.62), calls=%async_computation.5 | async-start | bytes 1048576 | tf_op jit(solution)/shard_map/all_to_all | solution.py:85
  152.1 1.1 copy.58
  153.3 1.0 reshape.189
  154.3 1.1 copy.73
  155.4 1.0 reshape.197
  156.4 0.1 copy.68
  156.5 1.0 reshape.195
  157.6 8.5 %all-to-all-done.5 = bf16[256,1,8,128]{3,2,1,0:T(8,128)(2,1)S(1)} async-done(((bf16[256,1,8,128]{3,2,1,0:T(8,128)(2,1)}), bf16[256,1,8,128]{3,2,1,0:T(8,128)(2,1)S(1)}, u32[]{:S(2)}, u32[]{:S(2)}) %all-to-all-start.5) | async-done | bytes 524320 | tf_op jit(solution)/shard_map/all_to_all | solution.py:85
  166.1 0.1 copy.63
  166.2 1.0 reshape.193
  (13 shorter events, 0.2 us)
Async XLA Ops:
  7.2 8.5 %copy-start.4 = (bf16[64,4096]{1,0:T(8,128)(2,1)S(1)}, bf16[64,4096]{1,0:T(8,128)(2,1)}, u32[]{:S(2)}) copy-start(bf16[64,4096]{1,0:T(8,128)(2,1)} %param.6) | copy-start | bytes 1572868
  9.4 20.8 %all-to-all-start.1 = ((bf16[64,4,8,128]{3,0,2,1:T(8,128)(2,1)}), bf16[64,4,8,128]{3,0,2,1:T(8,128)(2,1)S(1)}, u32[]{:S(2)}, u32[]{:S(2)}) async-start(bf16[64,4,8,128]{3,0,2,1:T(8,128)(2,1)} %copy.50), calls=%async_computation.1 | async-start | bytes 1048576 | tf_op jit(solution)/shard_map/all_to_all | solution.py:93
  30.2 17.4 %all-to-all-start.2 = ((bf16[64,4,8,128]{3,0,2,1:T(8,128)(2,1)}), bf16[64,4,8,128]{3,0,2,1:T(8,128)(2,1)S(1)}, u32[]{:S(2)}, u32[]{:S(2)}) async-start(bf16[64,4,8,128]{3,0,2,1:T(8,128)(2,1)} %copy.52), calls=%async_computation.2 | async-start | bytes 1048576 | tf_op jit(solution)/shard_map/all_to_all | solution.py:94
  33.7 54.2 %all-gather.5.cloned.1.call-start = ((), (), s32[]{:S(2)}) async-start(), calls=%async_computation.8 | async-start | bytes 2621440 | tf_op jit(solution)/shard_map/all_gather | solution.py:43
  33.7 15.1 %copy-start.5 = (bf16[64,4096]{1,0:T(8,128)(2,1)S(1)}, bf16[64,4096]{1,0:T(8,128)(2,1)}, u32[]{:S(2)}) copy-start(bf16[64,4096]{1,0:T(8,128)(2,1)} %param.4) | copy-start | bytes 1572868
  48.8 4.6 %copy-start.6 = (bf16[64,4096]{1,0:T(8,128)(2,1)S(1)}, bf16[64,4096]{1,0:T(8,128)(2,1)}, u32[]{:S(2)}) copy-start(bf16[64,4096]{1,0:T(8,128)(2,1)} %param.7) | copy-start | bytes 1572868
  49.9 17.4 %all-to-all-start = ((bf16[64,4,8,128]{3,0,2,1:T(8,128)(2,1)}), bf16[64,4,8,128]{3,0,2,1:T(8,128)(2,1)S(1)}, u32[]{:S(2)}, u32[]{:S(2)}) async-start(bf16[64,4,8,128]{3,0,2,1:T(8,128)(2,1)} %copy.48), calls=%async_computation | async-start | bytes 1048576 | tf_op jit(solution)/shard_map/all_to_all | solution.py:92
  67.4 17.4 %all-to-all-start.4 = ((bf16[64,4,8,128]{3,0,2,1:T(8,128)(2,1)}), bf16[64,4,8,128]{3,0,2,1:T(8,128)(2,1)S(1)}, u32[]{:S(2)}, u32[]{:S(2)}) async-start(bf16[64,4,8,128]{3,0,2,1:T(8,128)(2,1)} %copy.59), calls=%async_computation.4 | async-start | bytes 1048576 | tf_op jit(solution)/shard_map/all_to_all | solution.py:95
  70.8 37.0 %all-gather.7.cloned.1.call-start = ((), (), s32[]{:S(2)}) async-start(), calls=%async_computation.9 | async-start | bytes 2621440 | tf_op jit(solution)/shard_map/all_gather | solution.py:44
  87.9 1.9 %copy-start.1 = (f32[8,128,256]{1,2,0:T(8,128)S(1)}, f32[8,128,256]{1,2,0:T(8,128)}, u32[]{:S(2)}) copy-start(f32[8,128,256]{1,2,0:T(8,128)} %convolution_bitcast_fusion.3) | copy-start | bytes 3145732
  91.3 20.3 %all-to-all-start.3 = ((bf16[256,1,8,128]{3,2,1,0:T(8,128)(2,1)}), bf16[256,1,8,128]{3,2,1,0:T(8,128)(2,1)}, u32[]{:S(2)}, u32[]{:S(2)}) async-start(bf16[256,1,8,128]{3,2,1,0:T(8,128)(2,1)} %copy.57), calls=%async_computation.3 | async-start | bytes 1048576 | tf_op jit(solution)/shard_map/all_to_all | solution.py:84
  96.9 12.8 %copy-start = (f32[8,128,256]{1,2,0:T(8,128)S(1)}, f32[8,128,256]{1,2,0:T(8,128)}, u32[]{:S(2)}) copy-start(f32[8,128,256]{1,2,0:T(8,128)} %convolution_bitcast_fusion) | copy-start | bytes 3145732
  109.7 0.7 copy-start.2
  111.6 19.6 %all-to-all-start.7 = ((bf16[256,1,8,128]{3,2,1,0:T(8,128)(2,1)}), bf16[256,1,8,128]{3,2,1,0:T(8,128)(2,1)}, u32[]{:S(2)}, u32[]{:S(2)}) async-start(bf16[256,1,8,128]{3,2,1,0:T(8,128)(2,1)} %copy.72), calls=%async_computation.7 | async-start | bytes 1048576 | tf_op jit(solution)/shard_map/all_to_all | solution.py:87
  116.2 0.9 copy-start.3
  131.2 17.5 %all-to-all-start.6 = ((bf16[256,1,8,128]{3,2,1,0:T(8,128)(2,1)}), bf16[256,1,8,128]{3,2,1,0:T(8,128)(2,1)S(1)}, u32[]{:S(2)}, u32[]{:S(2)}) async-start(bf16[256,1,8,128]{3,2,1,0:T(8,128)(2,1)} %copy.67), calls=%async_computation.6 | async-start | bytes 1048576 | tf_op jit(solution)/shard_map/all_to_all | solution.py:86
  148.7 17.4 %all-to-all-start.5 = ((bf16[256,1,8,128]{3,2,1,0:T(8,128)(2,1)}), bf16[256,1,8,128]{3,2,1,0:T(8,128)(2,1)S(1)}, u32[]{:S(2)}, u32[]{:S(2)}) async-start(bf16[256,1,8,128]{3,2,1,0:T(8,128)(2,1)} %copy.62), calls=%async_computation.5 | async-start | bytes 1048576 | tf_op jit(solution)/shard_map/all_to_all | solution.py:85
Sparse Core Ops, SparseCore 0:
  49.0 21.6 all-gather.4
  86.1 21.6 all-gather.6
where the time goes:
time: 175 us; the launch traced here: 174 us
  waiting for transfers between devices  98.2 us (56%)
  starting transfers between devices  32.5 us (19%)
  local copies, waits for them, and re-layouts  17.1 us (10%)
  between operations  14.3 us (8%)
  matrix products  8.12 us (5%)
  other arithmetic  3.83 us (2%)
    all_to_all x1, waiting for transfers between devices, shards(): lax.all_to_all(to_heads(value_rows), 'head', split_axis=1, concat_axis=0,...  13.9 us
    all_to_all x1, waiting for transfers between devices, shards(): lax.all_to_all(to_heads(out_grad), 'head', split_axis=1, concat_axis=0, t...  13.9 us
    all_to_all x1, waiting for transfers between devices, shards(): lax.all_to_all(to_heads(key_rows), 'head', split_axis=1, concat_axis=0, t...  13.4 us
    all_to_all x1, waiting for transfers between devices, shards(): lax.all_to_all(to_heads(queries), 'head', split_axis=1, concat_axis=0, ti...  12.8 us
    all_to_all x1, waiting for transfers between devices, per_head(): lax.all_to_all(results[3], 'head', split_axis=0, concat_axis=1, tiled=True)  12.6 us
    all_to_all x1, waiting for transfers between devices, per_head(): lax.all_to_all(results[2], 'head', split_axis=0, concat_axis=1, tiled=True)  12.1 us
    all_gather x1, waiting for transfers between devices, per_head(): lax.all_gather(grad_total[None], 'seq', axis=0, tiled=True)  10.9 us
    all_to_all x1, waiting for transfers between devices, per_head(): lax.all_to_all(results[1], 'head', split_axis=0, concat_axis=1, tiled=True)  8.53 us
  transfers between devices with their start and end apart: 10, of which 8 were waited for; matrix products, arithmetic and copies ran while one was open for 14% of the time, Pallas kernels for 0%

commit v1 on v0

--- a/solution.py
+++ b/solution.py
@@ -5,6 +5,29 @@
 
 DH = 128
 BLK_MAX = 512
+
+
+def in_blocks(shard, dim, size):
+    lengths = shard.shape
+    pieces = shard.reshape(*lengths[:dim], size, lengths[dim] // size, *lengths[dim + 1 :])
+    return jnp.moveaxis(pieces, dim, 0)
+
+
+def joined_along(pieces, dim):
+    dims = list(pieces.shape[1:])
+    dims[dim] *= pieces.shape[0]
+    return jnp.moveaxis(pieces, 0, dim).reshape(dims)
+
+
+def swapped_with_each(x, axis, split_dim, concat_dim):
+    peers, index = (lax.axis_size(axis), lax.axis_index(axis))
+    blocks = in_blocks(x, split_dim, peers)
+    outs = [blocks[index]]
+    for hop in range(1, peers):
+        sent = blocks[index ^ hop]
+        outs.append(lax.ppermute(sent, axis, [(i, i ^ hop) for i in range(peers)]))
+    blocks = jnp.stack(outs)[index ^ jnp.arange(peers)]
+    return joined_along(blocks, concat_dim)
 
 
 def shards(queries, key_rows, value_rows, out_grad):
@@ -90,7 +113,7 @@
     outputs = per_head(
         (
             lax.all_to_all(to_heads(queries), "head", split_axis=1, concat_axis=0, tiled=True),
-            lax.all_to_all(to_heads(key_rows), "head", split_axis=1, concat_axis=0, tiled=True),
+            swapped_with_each(to_heads(key_rows), "head", 1, 0),
             lax.all_to_all(to_heads(value_rows), "head", split_axis=1, concat_axis=0, tiled=True),
             lax.all_to_all(to_heads(out_grad), "head", split_axis=1, concat_axis=0, tiled=True),
         )

time: 175 us -> 169 us (0.966)
  waiting for transfers between devices: 98.2 us -> 88.8 us
    ppermute x0 -> x3, waiting for transfers between devices: none -> 18.7 us  [swapped_with_each(): outs.append(lax.ppermute(sent, axis, [(i, i ^ hop) for i in range(peers)]))]
    all_to_all x1, waiting for transfers between devices: 13.9 us -> 0.01 us  [shards(): lax.all_to_all(to_heads(value_rows), 'head', split_axis=1, concat_axis=0,...]
    all_to_all x1 -> x0, waiting for transfers between devices: 13.4 us -> none  [shards(): lax.all_to_all(to_heads(key_rows), 'head', split_axis=1, concat_axis=0, t...]
    all_to_all x1, waiting for transfers between devices: 12.1 us -> 0.01 us  [per_head(): lax.all_to_all(results[2], 'head', split_axis=0, concat_axis=1, tiled=True)]
    all_gather x1, waiting for transfers between devices: 10.9 us -> 0.01 us  [per_head(): lax.all_gather(grad_total[None], 'seq', axis=0, tiled=True)]
    all_gather x1, waiting for transfers between devices: 0.01 us -> 9.53 us  [per_head(): lax.all_gather(kv_total[None], 'seq', axis=0, tiled=True)]
    all_to_all x1, waiting for transfers between devices: 0.01 us -> 8.53 us  [per_head(): lax.all_to_all(results[0], 'head', split_axis=0, concat_axis=1, tiled=True)]
    all_to_all x1 -> x0, starting transfers between devices: 6.32 us -> none  [shards(): lax.all_to_all(to_heads(key_rows), 'head', split_axis=1, concat_axis=0, t...]
  transfers between devices with their start and end apart: 10 -> 12, of which waited for: 8 -> 7; matrix products, arithmetic and copies ran while one was open for 14% -> 15% of each run, Pallas kernels for 0% -> 0%
where the time goes in v1:
time: 169 us; the launch traced here: 168 us
  waiting for transfers between devices  88.8 us (53%)
  starting transfers between devices  33.5 us (20%)
  local copies, waits for them, and re-layouts  18.1 us (11%)
  between operations  14.4 us (9%)
  matrix products  9.29 us (5%)
  other arithmetic  3.91 us (2%)
    ppermute x3, waiting for transfers between devices, swapped_with_each(): outs.append(lax.ppermute(sent, axis, [(i, i ^ hop) for i in range(peers)]))  18.7 us
    all_to_all x1, waiting for transfers between devices, shards(): lax.all_to_all(to_heads(out_grad), 'head', split_axis=1, concat_axis=0, t...  13.9 us
    all_to_all x1, waiting for transfers between devices, shards(): lax.all_to_all(to_heads(queries), 'head', split_axis=1, concat_axis=0, ti...  13.4 us
    all_to_all x1, waiting for transfers between devices, per_head(): lax.all_to_all(results[1], 'head', split_axis=0, concat_axis=1, tiled=True)  12.7 us
    all_to_all x1, waiting for transfers between devices, per_head(): lax.all_to_all(results[3], 'head', split_axis=0, concat_axis=1, tiled=True)  12.1 us
    all_gather x1, waiting for transfers between devices, per_head(): lax.all_gather(kv_total[None], 'seq', axis=0, tiled=True)  9.53 us
    all_to_all x1, waiting for transfers between devices, per_head(): lax.all_to_all(results[0], 'head', split_axis=0, concat_axis=1, tiled=True)  8.53 us
    all_to_all x1, starting transfers between devices, shards(): lax.all_to_all(to_heads(queries), 'head', split_axis=1, concat_axis=0, ti...  6.32 us
  transfers between devices with their start and end apart: 12, of which 7 were waited for; matrix products, arithmetic and copies ran while one was open for 15% of the time, Pallas kernels for 0%

profile of v1, /device:TPU:0, one launch (start us, length us, event | category | flops | bytes accessed | tf_op | source)
XLA Modules:
  0.0 168.0 jit_solution(13176079058529752644)
XLA Ops:
  7.2 1.2 copy.137
  8.4 1.0 copy.91
  9.4 6.3 %all-to-all-start = ((bf16[64,4,8,128]{3,0,2,1:T(8,128)(2,1)}), bf16[64,4,8,128]{3,0,2,1:T(8,128)(2,1)S(1)}, u32[]{:S(2)}, u32[]{:S(2)}) async-start(bf16[64,4,8,128]{3,0,2,1:T(8,128)(2,1)} %copy.91), calls=%async_computation | async-start | bytes 1048576 | tf_op jit(solution)/shard_map/all_to_all | solution.py:115
  15.7 0.1 copy.139
  15.8 1.0 copy.103
  16.8 13.4 %all-to-all-done = bf16[64,4,8,128]{3,0,2,1:T(8,128)(2,1)S(1)} async-done(((bf16[64,4,8,128]{3,0,2,1:T(8,128)(2,1)}), bf16[64,4,8,128]{3,0,2,1:T(8,128)(2,1)S(1)}, u32[]{:S(2)}, u32[]{:S(2)}) %all-to-all-start) | async-done | bytes 524320 | tf_op jit(solution)/shard_map/all_to_all | solution.py:115
  30.2 3.5 %all-to-all-start.3 = ((bf16[64,4,8,128]{3,0,2,1:T(8,128)(2,1)}), bf16[64,4,8,128]{3,0,2,1:T(8,128)(2,1)S(1)}, u32[]{:S(2)}, u32[]{:S(2)}) async-start(bf16[64,4,8,128]{3,0,2,1:T(8,128)(2,1)} %copy.103), calls=%async_computation.3 | async-start | bytes 1048576 | tf_op jit(solution)/shard_map/all_to_all | solution.py:118
  33.7 0.0 all-gather.7.cloned.1.call-start
  33.7 0.0 copy-start.6
  33.8 13.9 %all-to-all-done.3 = bf16[64,4,8,128]{3,0,2,1:T(8,128)(2,1)S(1)} async-done(((bf16[64,4,8,128]{3,0,2,1:T(8,128)(2,1)}), bf16[64,4,8,128]{3,0,2,1:T(8,128)(2,1)S(1)}, u32[]{:S(2)}, u32[]{:S(2)}) %all-to-all-start.3) | async-done | bytes 524320 | tf_op jit(solution)/shard_map/all_to_all | solution.py:118
  47.7 1.1 fusion.22
  48.8 0.0 all-gather.7.cloned.1.call-update
  48.8 0.1 copy.138
  48.9 1.0 copy.95
  49.9 3.5 %all-to-all-start.1 = ((bf16[64,4,8,128]{3,0,2,1:T(8,128)(2,1)}), bf16[64,4,8,128]{3,0,2,1:T(8,128)(2,1)S(1)}, u32[]{:S(2)}, u32[]{:S(2)}) async-start(bf16[64,4,8,128]{3,0,2,1:T(8,128)(2,1)} %copy.95), calls=%async_computation.1 | async-start | bytes 1048576 | tf_op jit(solution)/shard_map/all_to_all | solution.py:117
  53.4 0.0 all-gather.5.cloned.1.call-start
  53.5 0.1 copy.136
  53.6 0.1 dynamic-slice_bitcast_fusion.3
  53.7 2.9 %collective-permute-start.1 = (bf16[64,1,8,128]{3,2,0,1:T(8,128)(2,1)S(1)}, bf16[64,1,8,128]{3,2,0,1:T(8,128)(2,1)S(1)}, u32[]{:S(2)}, u32[]{:S(2)}) collective-permute-start(bf16[64,1,8,128]{3,2,0,1:T(8,128)(2,1)S(1)} %get-tuple-element.5), channel_id=1, source_target_pairs={{0,2},{1,3},{2,0},{3,1},{4,6},{5,7},{6,4},{7,5},{8,10},{9,11},{10,... | collective-permute-start | bytes 393224 | tf_op jit(solution)/shard_map/ppermute | solution.py:28
  56.6 1.5 collective-permute-start
  58.1 0.1 collective-permute-start.2
  58.2 18.7 %collective-permute-done.1 = bf16[64,1,8,128]{3,2,0,1:T(8,128)(2,1)S(1)} collective-permute-done((bf16[64,1,8,128]{3,2,0,1:T(8,128)(2,1)S(1)}, bf16[64,1,8,128]{3,2,0,1:T(8,128)(2,1)S(1)}, u32[]{:S(2)}, u32[]{:S(2)}) %collective-permute-start.1) | collective-permute-done | bytes 131104 | tf_op jit(solution)/shard_map/ppermute | solution.py:28
  76.9 0.1 maximum_bitcast_fusion
  76.9 0.6 gather_fusion
  77.6 0.3 copy.98
  77.9 0.0 all-to-all-done.1
  78.0 1.1 fusion.20
  79.1 0.0 all-gather.5.cloned.1.call-update
  79.1 0.4 select_convert_fusion
  79.6 1.0 copy-done
  80.6 1.4 convolution_bitcast_fusion.1
  82.0 1.9 %multiply_reduce_fusion = bf16[8,128,128]{2,1,0:T(8,128)(2,1)S(1)} fusion(f32[4,8,128,128]{3,2,1,0:T(8,128)} %bitcast.150, f32[4]{0:T(128)S(1)} %compare_convert_fusion), kind=kLoop, calls=%fused_computation.3 | loop fusion | flops 917504 | bytes 2359312 | tf_op jit(solution)/shard_map/reduce_sum | solution.py:74
  84.0 0.3 fusion.11
  84.3 1.1 copy.114
  85.4 4.1 %all-to-all-start.5 = ((bf16[256,1,8,128]{3,2,1,0:T(8,128)(2,1)}), bf16[256,1,8,128]{3,2,1,0:T(8,128)(2,1)}, u32[]{:S(2)}, u32[]{:S(2)}) async-start(bf16[256,1,8,128]{3,2,1,0:T(8,128)(2,1)} %copy.114), calls=%async_computation.5 | async-start | bytes 1048576 | tf_op jit(solution)/shard_map/all_to_all | solution.py:109
  89.6 2.7 %fusion.21 = f32[8,128,256]{1,2,0:T(8,128)} fusion(bf16[256,8,128]{0,2,1:T(8,128)(2,1)S(1)} %copy.98, bf16[8,256,256]{1,2,0:T(8,128)(2,1)} %copy-done), kind=kOutput, calls=%fused_computation.43 | convolution fusion | flops 134217728 | bytes 2621440 | tf_op jit(solution)/shard_map/bhts,bshd->bthd/dot_general | solution.py:88
  92.3 9.5 %all-gather.5.cloned.1.call-done = f32[32,128,128]{2,1,0:T(8,128)} async-done(((f32[8,128,128]{2,1,0:T(8,128)}), f32[32,128,128]{2,1,0:T(8,128)}) %all-gather.5.cloned.1.call-update) | async-done | bytes 2097168 | tf_op jit(solution)/shard_map/all_gather | solution.py:66
  101.8 1.9 %multiply_reduce_fusion.1 = bf16[8,128,128]{2,1,0:T(8,128)(2,1)S(1)} fusion(f32[4,8,128,128]{3,2,1,0:T(8,128)} %bitcast.151, f32[4]{0:T(128)S(1)} %compare_convert_fusion.1), kind=kLoop, calls=%fused_computation.5 | loop fusion | flops 917504 | bytes 2359312 | tf_op jit(solution)/shard_map/reduce_sum | solution.py:73
  103.6 0.0 copy-start.3
  103.7 0.3 fusion.12
  104.0 0.4 copy-done.3
  104.4 1.1 copy.110
  105.5 0.0 all-to-all-done.5
  105.5 4.6 %all-to-all-start.4 = ((bf16[256,1,8,128]{3,2,1,0:T(8,128)(2,1)}), bf16[256,1,8,128]{3,2,1,0:T(8,128)(2,1)}, u32[]{:S(2)}, u32[]{:S(2)}) async-start(bf16[256,1,8,128]{3,2,1,0:T(8,128)(2,1)} %copy.110), calls=%async_computation.4 | async-start | bytes 1048576 | tf_op jit(solution)/shard_map/all_to_all | solution.py:108
  110.1 0.4 fusion
  110.5 0.4 convolution_bitcast_fusion
  111.0 0.3 fusion.9
  111.3 1.1 copy.119
  112.4 12.7 %all-to-all-done.4 = bf16[256,1,8,128]{3,2,1,0:T(8,128)(2,1)} async-done(((bf16[256,1,8,128]{3,2,1,0:T(8,128)(2,1)}), bf16[256,1,8,128]{3,2,1,0:T(8,128)(2,1)}, u32[]{:S(2)}, u32[]{:S(2)}) %all-to-all-start.4) | async-done | bytes 524320 | tf_op jit(solution)/shard_map/all_to_all | solution.py:108
  125.1 3.5 %all-to-all-start.6 = ((bf16[256,1,8,128]{3,2,1,0:T(8,128)(2,1)}), bf16[256,1,8,128]{3,2,1,0:T(8,128)(2,1)S(1)}, u32[]{:S(2)}, u32[]{:S(2)}) async-start(bf16[256,1,8,128]{3,2,1,0:T(8,128)(2,1)} %copy.119), calls=%async_computation.6 | async-start | bytes 1048576 | tf_op jit(solution)/shard_map/all_to_all | solution.py:110
  128.6 0.5 convolution_bitcast_fusion.2
  129.1 0.3 fusion.10
  129.4 1.1 copy.101
  130.5 12.1 %all-to-all-done.6 = bf16[256,1,8,128]{3,2,1,0:T(8,128)(2,1)S(1)} async-done(((bf16[256,1,8,128]{3,2,1,0:T(8,128)(2,1)}), bf16[256,1,8,128]{3,2,1,0:T(8,128)(2,1)S(1)}, u32[]{:S(2)}, u32[]{:S(2)}) %all-to-all-start.6) | async-done | bytes 524320 | tf_op jit(solution)/shard_map/all_to_all | solution.py:110
  142.6 3.5 %all-to-all-start.2 = ((bf16[256,1,8,128]{3,2,1,0:T(8,128)(2,1)}), bf16[256,1,8,128]{3,2,1,0:T(8,128)(2,1)S(1)}, u32[]{:S(2)}, u32[]{:S(2)}) async-start(bf16[256,1,8,128]{3,2,1,0:T(8,128)(2,1)} %copy.101), calls=%async_computation.2 | async-start | bytes 1048576 | tf_op jit(solution)/shard_map/all_to_all | solution.py:107
  146.1 1.1 copy.115
  147.2 1.0 reshape.210
  148.2 1.1 copy.111
  149.4 1.0 reshape.208
  150.4 0.1 copy.120
  150.5 1.0 reshape.212
  151.5 8.5 %all-to-all-done.2 = bf16[256,1,8,128]{3,2,1,0:T(8,128)(2,1)S(1)} async-done(((bf16[256,1,8,128]{3,2,1,0:T(8,128)(2,1)}), bf16[256,1,8,128]{3,2,1,0:T(8,128)(2,1)S(1)}, u32[]{:S(2)}, u32[]{:S(2)}) %all-to-all-start.2) | async-done | bytes 524320 | tf_op jit(solution)/shard_map/all_to_all | solution.py:107
  160.0 0.1 copy.102
  160.1 1.0 reshape.204
  (23 shorter events, 0.2 us)
Async XLA Ops:
  7.2 8.5 %copy-start.5 = (bf16[64,4096]{1,0:T(8,128)(2,1)S(1)}, bf16[64,4096]{1,0:T(8,128)(2,1)}, u32[]{:S(2)}) copy-start(bf16[64,4096]{1,0:T(8,128)(2,1)} %param.7) | copy-start | bytes 1572868
  9.4 20.8 %all-to-all-start = ((bf16[64,4,8,128]{3,0,2,1:T(8,128)(2,1)}), bf16[64,4,8,128]{3,0,2,1:T(8,128)(2,1)S(1)}, u32[]{:S(2)}, u32[]{:S(2)}) async-start(bf16[64,4,8,128]{3,0,2,1:T(8,128)(2,1)} %copy.91), calls=%async_computation | async-start | bytes 1048576 | tf_op jit(solution)/shard_map/all_to_all | solution.py:115
  30.2 17.4 %all-to-all-start.3 = ((bf16[64,4,8,128]{3,0,2,1:T(8,128)(2,1)}), bf16[64,4,8,128]{3,0,2,1:T(8,128)(2,1)S(1)}, u32[]{:S(2)}, u32[]{:S(2)}) async-start(bf16[64,4,8,128]{3,0,2,1:T(8,128)(2,1)} %copy.103), calls=%async_computation.3 | async-start | bytes 1048576 | tf_op jit(solution)/shard_map/all_to_all | solution.py:118
  33.7 48.3 %all-gather.7.cloned.1.call-start = ((), (), s32[]{:S(2)}) async-start(), calls=%async_computation.8 | async-start | bytes 2621440 | tf_op jit(solution)/shard_map/all_gather | solution.py:67
  33.7 15.1 %copy-start.6 = (bf16[64,4096]{1,0:T(8,128)(2,1)S(1)}, bf16[64,4096]{1,0:T(8,128)(2,1)}, u32[]{:S(2)}) copy-start(bf16[64,4096]{1,0:T(8,128)(2,1)} %param.6) | copy-start | bytes 1572868
  48.8 4.7 %copy-start.7 = (bf16[64,4096]{1,0:T(8,128)(2,1)S(1)}, bf16[64,4096]{1,0:T(8,128)(2,1)}, u32[]{:S(2)}) copy-start(bf16[64,4096]{1,0:T(8,128)(2,1)} %param.5) | copy-start | bytes 1572868
  49.9 28.0 %all-to-all-start.1 = ((bf16[64,4,8,128]{3,0,2,1:T(8,128)(2,1)}), bf16[64,4,8,128]{3,0,2,1:T(8,128)(2,1)S(1)}, u32[]{:S(2)}, u32[]{:S(2)}) async-start(bf16[64,4,8,128]{3,0,2,1:T(8,128)(2,1)} %copy.95), calls=%async_computation.1 | async-start | bytes 1048576 | tf_op jit(solution)/shard_map/all_to_all | solution.py:117
  53.4 48.4 %all-gather.5.cloned.1.call-start = ((), (), s32[]{:S(2)}) async-start(), calls=%async_computation.7 | async-start | bytes 2621440 | tf_op jit(solution)/shard_map/all_gather | solution.py:66
  53.7 23.1 %collective-permute-start.1 = (bf16[64,1,8,128]{3,2,0,1:T(8,128)(2,1)S(1)}, bf16[64,1,8,128]{3,2,0,1:T(8,128)(2,1)S(1)}, u32[]{:S(2)}, u32[]{:S(2)}) collective-permute-start(bf16[64,1,8,128]{3,2,0,1:T(8,128)(2,1)S(1)} %get-tuple-element.5), channel_id=1, source_target_pairs={{0,2},{1,3},{2,0},{3,1},{4,6},{5,7},{6,4},{7,5},{8,10},{9,11},{10,... | collective-permute-start | bytes 393224 | tf_op jit(solution)/shard_map/ppermute | solution.py:28
  56.6 20.3 %collective-permute-start = (bf16[64,1,8,128]{3,2,0,1:T(8,128)(2,1)S(1)}, bf16[64,1,8,128]{3,2,0,1:T(8,128)(2,1)S(1)}, u32[]{:S(2)}, u32[]{:S(2)}) collective-permute-start(bf16[64,1,8,128]{3,2,0,1:T(8,128)(2,1)S(1)} %get-tuple-element.6), channel_id=1, source_target_pairs={{0,1},{1,0},{2,3},{3,2},{4,5},{5,4},{6,7},{7,6},{8,9},{9,8},{10,11... | collective-permute-start | bytes 393224 | tf_op jit(solution)/shard_map/ppermute | solution.py:28
  58.1 18.8 %collective-permute-start.2 = (bf16[64,1,8,128]{3,2,0,1:T(8,128)(2,1)S(1)}, bf16[64,1,8,128]{3,2,0,1:T(8,128)(2,1)S(1)}, u32[]{:S(2)}, u32[]{:S(2)}) collective-permute-start(bf16[64,1,8,128]{3,2,0,1:T(8,128)(2,1)S(1)} %get-tuple-element.7), channel_id=1, source_target_pairs={{0,3},{1,2},{2,1},{3,0},{4,7},{5,6},{6,5},{7,4},{8,11},{9,10},{10,... | collective-permute-start | bytes 393224 | tf_op jit(solution)/shard_map/ppermute | solution.py:28
  79.6 1.0 copy-start
  82.0 1.9 %copy-start.2 = (f32[8,128,256]{1,2,0:T(8,128)S(1)}, f32[8,128,256]{1,2,0:T(8,128)}, u32[]{:S(2)}) copy-start(f32[8,128,256]{1,2,0:T(8,128)} %convolution_bitcast_fusion.1) | copy-start | bytes 3145732
  85.4 20.1 %all-to-all-start.5 = ((bf16[256,1,8,128]{3,2,1,0:T(8,128)(2,1)}), bf16[256,1,8,128]{3,2,1,0:T(8,128)(2,1)}, u32[]{:S(2)}, u32[]{:S(2)}) async-start(bf16[256,1,8,128]{3,2,1,0:T(8,128)(2,1)} %copy.114), calls=%async_computation.5 | async-start | bytes 1048576 | tf_op jit(solution)/shard_map/all_to_all | solution.py:109
  92.3 11.4 %copy-start.1 = (f32[8,128,256]{1,2,0:T(8,128)S(1)}, f32[8,128,256]{1,2,0:T(8,128)}, u32[]{:S(2)}) copy-start(f32[8,128,256]{1,2,0:T(8,128)} %fusion.21) | copy-start | bytes 3145732
  103.6 0.7 copy-start.3
  105.5 19.6 %all-to-all-start.4 = ((bf16[256,1,8,128]{3,2,1,0:T(8,128)(2,1)}), bf16[256,1,8,128]{3,2,1,0:T(8,128)(2,1)}, u32[]{:S(2)}, u32[]{:S(2)}) async-start(bf16[256,1,8,128]{3,2,1,0:T(8,128)(2,1)} %copy.110), calls=%async_computation.4 | async-start | bytes 1048576 | tf_op jit(solution)/shard_map/all_to_all | solution.py:108
  112.4 16.7 %copy-start.4 = (bf16[8,128,128]{2,1,0:T(8,128)(2,1)S(1)}, bf16[8,128,128]{2,1,0:T(8,128)(2,1)}, u32[]{:S(2)}) copy-start(bf16[8,128,128]{2,1,0:T(8,128)(2,1)} %copy-done.3) | copy-start | bytes 786436
  125.1 17.5 %all-to-all-start.6 = ((bf16[256,1,8,128]{3,2,1,0:T(8,128)(2,1)}), bf16[256,1,8,128]{3,2,1,0:T(8,128)(2,1)S(1)}, u32[]{:S(2)}, u32[]{:S(2)}) async-start(bf16[256,1,8,128]{3,2,1,0:T(8,128)(2,1)} %copy.119), calls=%async_computation.6 | async-start | bytes 1048576 | tf_op jit(solution)/shard_map/all_to_all | solution.py:110
  142.6 17.4 %all-to-all-start.2 = ((bf16[256,1,8,128]{3,2,1,0:T(8,128)(2,1)}), bf16[256,1,8,128]{3,2,1,0:T(8,128)(2,1)S(1)}, u32[]{:S(2)}, u32[]{:S(2)}) async-start(bf16[256,1,8,128]{3,2,1,0:T(8,128)(2,1)} %copy.101), calls=%async_computation.2 | async-start | bytes 1048576 | tf_op jit(solution)/shard_map/all_to_all | solution.py:107
Sparse Core Ops, SparseCore 0:
  49.0 21.6 all-gather.6
  79.2 22.5 all-gather.4
